TPU v7x, 512 devices: a whole 4x8x8 slice. The times are simulated.
512 devices in a mesh: shot: 16 (over x_lo, z), tile: 32 (over y, x_hi, core).
Axes of the slice: x: 4 (x_hi: 2, x_lo: 2; x = x_hi * 2 + x_lo), y: 8, z: 8, core: 2. Of those that a mesh axis runs over, the one named last changes fastest.
Arguments:
- latent: bfloat16 [96, 16, 64, 64], P('tile', 'shot'), may hold values from -6 to 6
- kernel: bfloat16 [27, 64, 64], replicated, may hold values from -0.15625 to 0.15625
- conv_bias: float32 [64], replicated, may hold values from -3 to 3
- head_weight: bfloat16 [64], replicated, may hold values from -0.75 to 0.75
- density: float32 [192, 32, 128], P('tile'), may hold values from 1 to 2.5
- wave_prev: float32 [16, 192, 32, 128], P('shot', 'tile'), may hold values from -6 to 6
- wave_now: float32 [16, 192, 32, 128], P('shot', 'tile'), may hold values from -6 to 6
- adjoint_next: float32 [16, 192, 32, 128], P('shot', 'tile'), may hold values from -6 to 6
- adjoint_after: float32 [16, 192, 32, 128], P('shot', 'tile'), may hold values from -6 to 6
- source_cell: int32 [16], P('shot'), may hold values from 0 to 786431
- wavelet: float32 [16, 3], P('shot'), may hold values from -24 to 24
- receiver_cells: int32 [16, 128], P('shot'), may hold values from 0 to 786431
- observed: float32 [16, 3, 128], P('shot'), may hold values from -6 to 6
Outputs:
- latent_grad: float32 [96, 16, 64, 64], P('tile', 'shot')
- kernel_grad: float32 [27, 64, 64], replicated
- head_grad: float32 [64], replicated
- bias_grad: float32 [64], replicated
All inputs are finite; a program needn't handle non-finite values.
Results may differ from a plain program's by a relative error of at most 0.0034.
The roundings to bfloat16 on the way count: a program that leaves them out, or rounds other values in their place, can miss the bound.
Values may be sent and summed in bfloat16 or wider, within the bound.
No kernel may reach another device: no remote copies, remote signals or barrier semaphores. Data moves between devices by JAX's collectives and lax.ppermute only.
A program may use at most 64 MiB of HBM per device.

v0:
```python
import jax
import jax.numpy as jnp
from jax import lax
from jax.sharding import PartitionSpec as P

courant = 0.005
speed_low = 1.5
speed_span = 3.0


def padded_2(cells, sides, width):
    for axis, dim in sides:
        count = lax.axis_size(axis)
        ends = count - 1
        head = lax.slice_in_dim(cells, 0, width, axis=dim)
        tail = lax.slice_in_dim(cells, cells.shape[dim] - width, cells.shape[dim], axis=dim)
        cells = jnp.concatenate(
            [
                lax.ppermute(tail, axis, [(i, (i + 1) % count) for i in range(ends)]),
                cells,
                lax.ppermute(head, axis, [((i + 1) % count, i) for i in range(ends)]),
            ],
            axis=dim,
        )
    return cells


def upsample(coarse):
    coarse_x, coarse_z, channels, coarse_y = coarse.shape
    spread = jnp.broadcast_to(
        coarse[:, None, :, None, :, :, None], (coarse_x, 2, coarse_z, 2, channels, coarse_y, 2)
    )
    return spread.reshape(coarse_x * 2, coarse_z * 2, channels, coarse_y * 2)


def fold_children(fine):
    fine_x, fine_z, channels, fine_y = fine.shape
    grouped = fine.reshape(fine_x // 2, 2, fine_z // 2, 2, channels, fine_y // 2, 2)
    return jnp.sum(grouped, axis=(1, 3, 6))


def shifted_stack(padded, start_x, start_z, starts_y, cells_x, cells_z, cells_y):
    return jnp.concatenate(
        [
            padded[
                start_x : start_x + cells_x,
                start_z : start_z + cells_z,
                :,
                start_y : start_y + cells_y,
            ]
            for start_y in starts_y
        ],
        axis=2,
    )


def convolve(padded, kernel):
    cells_x = padded.shape[0] - 2
    cells_z = padded.shape[1] - 2
    channels = padded.shape[2]
    cells_y = padded.shape[3] - 2
    tap_table = kernel.reshape(3, 3, 3, channels, channels)
    result = jnp.zeros((cells_x, cells_z, channels, cells_y), jnp.float32)
    for offset_x in range(3):
        for offset_z in range(3):
            stacked = shifted_stack(
                padded, offset_x, offset_z, (0, 1, 2), cells_x, cells_z, cells_y
            )
            matrix = jnp.transpose(tap_table[offset_x, offset_z], (1, 0, 2)).reshape(
                channels, 3 * channels
            )
            result = result + jnp.einsum(
                "ok,abky->aboy", matrix, stacked, preferred_element_type=jnp.float32
            )
    return result


def kernel_terms(padded, grad_low):
    cells_x, cells_z, channels, cells_y = grad_low.shape
    pieces = []
    for offset_x in range(3):
        for offset_z in range(3):
            stacked = shifted_stack(
                padded, offset_x, offset_z, (0, 1, 2), cells_x, cells_z, cells_y
            )
            product = jnp.einsum(
                "aboy,abky->ok", grad_low, stacked, preferred_element_type=jnp.float32
            )
            pieces.append(jnp.transpose(product.reshape(channels, 3, channels), (1, 0, 2)))
    return jnp.stack(pieces).reshape(27, channels, channels)


def transposed(grad_padded, kernel):
    cells_x = grad_padded.shape[0] - 2
    cells_z = grad_padded.shape[1] - 2
    channels = grad_padded.shape[2]
    cells_y = grad_padded.shape[3] - 2
    tap_table = kernel.reshape(3, 3, 3, channels, channels)
    result = jnp.zeros((cells_x, cells_z, channels, cells_y), jnp.float32)
    for offset_x in range(3):
        for offset_z in range(3):
            stacked = shifted_stack(
                grad_padded, 2 - offset_x, 2 - offset_z, (2, 1, 0), cells_x, cells_z, cells_y
            )
            matrix = tap_table[offset_x, offset_z].reshape(3 * channels, channels)
            result = result + jnp.einsum(
                "kc,abky->abcy", matrix, stacked, preferred_element_type=jnp.float32
            )
    return result


def neighbours(padded):
    return (
        padded[2:, 1:-1, 1:-1],
        padded[:-2, 1:-1, 1:-1],
        padded[1:-1, 2:, 1:-1],
        padded[1:-1, :-2, 1:-1],
        padded[1:-1, 1:-1, 2:],
        padded[1:-1, 1:-1, :-2],
    )


def face_weights(padded_buoyancy):
    centre = padded_buoyancy[1:-1, 1:-1, 1:-1]
    return tuple((0.5 * (centre + beside) for beside in neighbours(padded_buoyancy)))


def apply_faces(padded, faces):
    centre = padded[1:-1, 1:-1, 1:-1]
    result = jnp.zeros_like(centre)
    for weight, beside in zip(faces, neighbours(padded)):
        result = result + weight * (beside - centre)
    return result


def propagate(
    laplace,
    coefficient,
    previous,
    current,
    following,
    beyond,
    anchor,
    source_cell,
    wavelet,
    receiver_cells,
    observed,
):
    field_shape = previous.shape
    field_cells = previous.size
    source_local = source_cell[0] - anchor
    source_owned = jnp.logical_and(source_local >= 0, source_local < field_cells).astype(
        jnp.float32
    )
    source_spot = jnp.clip(source_local, 0, field_cells - 1)
    receiver_local = receiver_cells[0] - anchor
    receiver_owned = jnp.logical_and(receiver_local >= 0, receiver_local < field_cells).astype(
        jnp.float32
    )
    receiver_spot = jnp.clip(receiver_local, 0, field_cells - 1)
    count_steps = wavelet.shape[1]
    laplacians = []
    residuals = []
    for instant in range(count_steps):
        laplacian = laplace(current)
        laplacians.append(laplacian)
        advanced = 2.0 * current - previous + coefficient * laplacian
        advanced = (
            advanced.reshape(-1)
            .at[source_spot]
            .add(source_owned * wavelet[0, instant])
            .reshape(field_shape)
        )
        residuals.append(
            receiver_owned * (advanced.reshape(-1)[receiver_spot] - observed[0, instant])
        )
        previous, current = (current, advanced)
    laplacians.append(laplace(current))
    coef_grad = following * laplacians[count_steps]
    for instant in reversed(range(count_steps)):
        preceding = 2.0 * following - beyond + laplace(coefficient * following)
        preceding = (
            preceding.reshape(-1).at[receiver_spot].add(residuals[instant]).reshape(field_shape)
        )
        coef_grad = coef_grad + preceding * laplacians[instant]
        beyond, following = (following, preceding)
    return coef_grad


def per_device(
    latent,
    kernel,
    conv_bias,
    head_weight,
    density,
    wave_prev,
    wave_now,
    adjoint_next,
    adjoint_after,
    source_cell,
    wavelet,
    receiver_cells,
    observed,
):
    extended = padded_2(upsample(latent), (("shot", 1), ("tile", 0)), 1)
    padded = jnp.pad(extended, ((0, 0), (0, 0), (0, 0), (1, 1)))
    pre_act = convolve(padded, kernel) + conv_bias[None, None, :, None]
    hidden = jax.nn.silu(pre_act).astype(jnp.bfloat16)
    logit = jnp.einsum("abcy,c->aby", hidden, head_weight, preferred_element_type=jnp.float32)
    squash = jax.nn.sigmoid(logit)
    velocity = speed_low + speed_span * squash
    tile_speed = lax.all_gather(velocity, "shot", axis=1, tiled=True)
    tile_cells = tile_speed.size
    buoyancy = 1.0 / density
    coefficient = courant * tile_speed * tile_speed * density
    factor = 2.0 * courant * tile_speed * density
    buoyancy_edges = padded_2(buoyancy, (("tile", 0),), 1)
    faces = face_weights(jnp.pad(buoyancy_edges, ((0, 0), (1, 1), (1, 1))))

    def laplace(field):
        field_edges = padded_2(field, (("tile", 0),), 1)
        return apply_faces(jnp.pad(field_edges, ((0, 0), (1, 1), (1, 1))), faces)

    anchor = lax.axis_index("tile") * tile_cells
    coef_grad = propagate(
        laplace,
        coefficient,
        wave_prev[0],
        wave_now[0],
        adjoint_next[0],
        adjoint_after[0],
        anchor,
        source_cell,
        wavelet,
        receiver_cells,
        observed,
    )
    strip_grad = lax.psum_scatter(coef_grad * factor, "shot", scatter_dimension=1, tiled=True)
    logit_grad = strip_grad * speed_span * squash * (1.0 - squash)
    head_part = jnp.einsum(
        "abcy,aby->c", hidden.astype(jnp.float32), logit_grad, precision=lax.Precision.HIGHEST
    )
    gate = jax.nn.sigmoid(pre_act)
    pre_grad = (
        logit_grad[:, :, None, :]
        * head_weight.astype(jnp.float32)[None, None, :, None]
        * (gate * (1.0 + pre_act * (1.0 - gate)))
    )
    bias_part = jnp.sum(pre_grad, axis=(0, 1, 3))
    grad_low = pre_grad.astype(jnp.bfloat16)
    kernel_part = kernel_terms(padded, grad_low)
    grad_edges = padded_2(grad_low, (("shot", 1), ("tile", 0)), 1)
    grad_padded = jnp.pad(grad_edges, ((0, 0), (0, 0), (0, 0), (1, 1)))
    latent_grad = fold_children(transposed(grad_padded, kernel))
    kernel_grad, head_grad, bias_grad = lax.psum(
        (kernel_part, head_part, bias_part), ("shot", "tile")
    )
    return (latent_grad, kernel_grad, head_grad, bias_grad)


def solution(mesh):
    return jax.shard_map(
        per_device,
        mesh=mesh,
        in_specs=(
            P("tile", "shot", None, None),
            P(),
            P(),
            P(),
            P("tile", None, None),
            P("shot", "tile", None, None),
            P("shot", "tile", None, None),
            P("shot", "tile", None, None),
            P("shot", "tile", None, None),
            P("shot"),
            P("shot", None),
            P("shot", None),
            P("shot", None, None),
        ),
        out_specs=(P("tile", "shot", None, None), P(), P(), P()),
        check_vma=False,
    )
```

profile of v0, /device:TPU:1, one launch (start us, length us, event | category | flops | bytes accessed | tf_op | source)
XLA Modules:
  0.0 589.9 jit_solution(18035886360403443610)
XLA Ops:
  8.4 4.8 collective-permute-start.1
  15.3 5.2 collective-permute-start.5
  20.5 2.2 collective-permute-start.7
  26.8 2.4 collective-permute-start.3
  29.2 1.9 collective-permute-start.4
  31.4 5.0 collective-permute-done.4
  42.4 32.4 %all_gather.3 = f32[6,32,128]{2,0,1:T(8,128)S(1)} all-gather(f32[6,2,128]{2,0,1:T(8,128)S(1)} %multiply_add_fusion.2), channel_id=1, replica_groups=mesh['shot'=16,'tile'=32] {'shot'}, dimensions={1}, use_global_device_ids=true | all-gather | bytes 104448 | tf_op jit(solution)/shard_map/all_gather | solution.py:212
  74.9 5.3 collective-permute-start
  80.3 6.1 %collective-permute-start.6 = (f32[1,32,128]{2,1,0:T(8,128)S(1)}, f32[1,32,128]{2,1,0:T(8,128)S(1)}, u32[]{:S(2)}, u32[]{:S(2)}) collective-permute-start(f32[1,32,128]{2,1,0:T(8,128)S(1)} %get-tuple-element.149), channel_id=1, source_target_pairs={{0,1},{1,2},{2,3},{3,4},{4,5},{5,6},{6,7},{7,8},{8,9},{9,10},{10,1... | collective-permute-start | bytes 49160 | tf_op jit(solution)/shard_map/ppermute | solution.py:19
  86.4 1.9 collective-permute-start.14
  88.4 5.1 collective-permute-start.15
  97.1 5.7 collective-permute-start.9
  106.1 5.7 collective-permute-start.11
  120.0 5.1 collective-permute-start.17
  127.1 5.1 collective-permute-start.13
  134.1 1.9 collective-permute-start.18
  136.0 5.5 collective-permute-start.19
  147.3 136.4 %all-reduce.17.cloned.1.call-done = f32[6,32,128]{2,1,0:T(8,128)} async-done(((f32[6,32,128]{2,1,0:T(8,128)}), f32[6,32,128]{2,1,0:T(8,128)}) %all-reduce.17.cloned.1.call-update) | async-done | bytes 98320
  297.0 2.1 collective-permute-done.21
  299.1 16.4 %collective-permute-start.22 = (bf16[1,4,64,128]{3,2,1,0:T(8,128)(2,1)S(1)}, bf16[1,4,64,128]{3,2,1,0:T(8,128)(2,1)S(1)}, u32[]{:S(2)}, u32[]{:S(2)}) collective-permute-start(bf16[1,4,64,128]{3,2,1,0:T(8,128)(2,1)S(1)} %get-tuple-element.129), channel_id=1, source_target_pairs={{0,1},{1,2},{2,3},{3,4},{4,5},{5,6},{6,7},{7,8},{8,9},{9,10},{10,1... | collective-permute-start | bytes 196616 | tf_op jit(solution)/shard_map/ppermute | solution.py:19
  315.5 1.9 collective-permute-start.23
  317.7 101.0 %all-reduce.11 = (f32[64]{0:T(128)}, f32[64]{0:T(128)}) all-reduce(f32[64]{0:T(128)S(1)} %convolution_bitcast_fusion, f32[64]{0:T(128)S(1)} %get-tuple-element.46), channel_id=1, replica_groups=mesh['shot'=16,'tile'=32] {'shot','tile'}, use_global_device_ids=true, to_apply=%region_7.8 | all-reduce | flops 128 | bytes 1024 | tf_op jit(solution)/shard_map/psum | solution.py:255
  426.6 154.3 %all-reduce.15.cloned.1.call-done = f32[27,64,64]{2,1,0:T(8,128)} async-done(((f32[27,64,64]{2,1,0:T(8,128)}), f32[27,64,64]{2,1,0:T(8,128)}) %all-reduce.15.cloned.1.call-update) | async-done | bytes 442384 | tf_op jit(solution)/shard_map/psum | solution.py:255
  580.9 2.2 copy.315
  (264 shorter events, 55.1 us)
Async XLA Ops:
  7.2 276.4 %all-reduce.17.cloned.1.call-start = ((), (), s32[]{:S(2)}) async-start(), calls=%async_computation.1 | async-start | bytes 196608
  8.4 18.3 %collective-permute-start.1 = (bf16[6,1,64,128]{3,2,1,0:T(8,128)(2,1)S(1)}, bf16[6,1,64,128]{3,2,1,0:T(8,128)(2,1)S(1)}, u32[]{:S(2)}, u32[]{:S(2)}) collective-permute-start(bf16[6,1,64,128]{3,2,1,0:T(8,128)(2,1)S(1)} %copy.176), channel_id=1, source_target_pairs={{0,32},{32,64},{64,96},{96,128},{128,160},{160,192},{192,224},{224... | collective-permute-start | bytes 294920 | tf_op jit(solution)/shard_map/ppermute | solution.py:19
  13.2 13.5 %collective-permute-start.2 = (bf16[6,1,64,128]{3,2,1,0:T(8,128)(2,1)S(1)}, bf16[6,1,64,128]{3,2,1,0:T(8,128)(2,1)S(1)}, u32[]{:S(2)}, u32[]{:S(2)}) collective-permute-start(bf16[6,1,64,128]{3,2,1,0:T(8,128)(2,1)S(1)} %copy.176), channel_id=1, source_target_pairs={{32,0},{64,32},{96,64},{128,96},{160,128},{192,160},{224,192},{256... | collective-permute-start | bytes 294920 | tf_op jit(solution)/shard_map/ppermute | solution.py:21
  15.3 15.9 %collective-permute-start.5 = (f32[1,32,128]{2,1,0:T(8,128)S(1)}, f32[1,32,128]{2,1,0:T(8,128)S(1)}, u32[]{:S(2)}, u32[]{:S(2)}) collective-permute-start(f32[1,32,128]{2,1,0:T(8,128)S(1)} %get-tuple-element.148), channel_id=1, source_target_pairs={{1,0},{2,1},{3,2},{4,3},{5,4},{6,5},{7,6},{8,7},{9,8},{10,9},{11,1... | collective-permute-start | bytes 49160 | tf_op jit(solution)/shard_map/ppermute | solution.py:21
  20.5 10.6 %collective-permute-start.7 = (f32[1,32,128]{2,1,0:T(8,128)S(1)}, f32[1,32,128]{2,1,0:T(8,128)S(1)}, u32[]{:S(2)}, u32[]{:S(2)}) collective-permute-start(f32[1,32,128]{2,1,0:T(8,128)S(1)} %get-tuple-element.147), channel_id=1, source_target_pairs={{0,1},{1,2},{2,3},{3,4},{4,5},{5,6},{6,7},{7,8},{8,9},{9,10},{10,1... | collective-permute-start | bytes 49160 | tf_op jit(solution)/shard_map/ppermute | solution.py:19
  29.2 7.1 %collective-permute-start.4 = (bf16[1,4,64,128]{3,2,1,0:T(8,128)(2,1)S(1)}, bf16[1,4,64,128]{3,2,1,0:T(8,128)(2,1)S(1)}, u32[]{:S(2)}, u32[]{:S(2)}) collective-permute-start(bf16[1,4,64,128]{3,2,1,0:T(8,128)(2,1)S(1)} %get-tuple-element.134), channel_id=1, source_target_pairs={{1,0},{2,1},{3,2},{4,3},{5,4},{6,5},{7,6},{8,7},{9,8},{10,9},{11,1... | collective-permute-start | bytes 196616 | tf_op jit(solution)/shard_map/ppermute | solution.py:21
  74.9 18.6 %collective-permute-start = (f32[1,32,128]{2,1,0:T(8,128)S(1)}, f32[1,32,128]{2,1,0:T(8,128)S(1)}, u32[]{:S(2)}, u32[]{:S(2)}) collective-permute-start(f32[1,32,128]{2,1,0:T(8,128)S(1)} %get-tuple-element.150), channel_id=1, source_target_pairs={{1,0},{2,1},{3,2},{4,3},{5,4},{6,5},{7,6},{8,7},{9,8},{10,9},{11,1... | collective-permute-start | bytes 49160 | tf_op jit(solution)/shard_map/ppermute | solution.py:21
  80.3 13.3 %collective-permute-start.6 = (f32[1,32,128]{2,1,0:T(8,128)S(1)}, f32[1,32,128]{2,1,0:T(8,128)S(1)}, u32[]{:S(2)}, u32[]{:S(2)}) collective-permute-start(f32[1,32,128]{2,1,0:T(8,128)S(1)} %get-tuple-element.149), channel_id=1, source_target_pairs={{0,1},{1,2},{2,3},{3,4},{4,5},{5,6},{6,7},{7,8},{8,9},{9,10},{10,1... | collective-permute-start | bytes 49160 | tf_op jit(solution)/shard_map/ppermute | solution.py:19
  86.4 7.3 %collective-permute-start.14 = (f32[1,32,128]{2,1,0:T(8,128)S(1)}, f32[1,32,128]{2,1,0:T(8,128)S(1)}, u32[]{:S(2)}, u32[]{:S(2)}) collective-permute-start(f32[1,32,128]{2,1,0:T(8,128)S(1)} %get-tuple-element.153), channel_id=1, source_target_pairs={{1,0},{2,1},{3,2},{4,3},{5,4},{6,5},{7,6},{8,7},{9,8},{10,9},{11,1... | collective-permute-start | bytes 49160 | tf_op jit(solution)/shard_map/ppermute | solution.py:21
  88.4 6.0 %collective-permute-start.15 = (f32[1,32,128]{2,1,0:T(8,128)S(1)}, f32[1,32,128]{2,1,0:T(8,128)S(1)}, u32[]{:S(2)}, u32[]{:S(2)}) collective-permute-start(f32[1,32,128]{2,1,0:T(8,128)S(1)} %get-tuple-element.152), channel_id=1, source_target_pairs={{0,1},{1,2},{2,3},{3,4},{4,5},{5,6},{6,7},{7,8},{8,9},{9,10},{10,1... | collective-permute-start | bytes 49160 | tf_op jit(solution)/shard_map/ppermute | solution.py:19
  95.2 8.3 %collective-permute-start.8 = (f32[1,32,128]{2,1,0:T(8,128)S(1)}, f32[1,32,128]{2,1,0:T(8,128)S(1)}, u32[]{:S(2)}, u32[]{:S(2)}) collective-permute-start(f32[1,32,128]{2,1,0:T(8,128)S(1)} %get-tuple-element.146), channel_id=1, source_target_pairs={{1,0},{2,1},{3,2},{4,3},{5,4},{6,5},{7,6},{8,7},{9,8},{10,9},{11,1... | collective-permute-start | bytes 49160 | tf_op jit(solution)/shard_map/ppermute | solution.py:21
  97.1 6.6 %collective-permute-start.9 = (f32[1,32,128]{2,1,0:T(8,128)S(1)}, f32[1,32,128]{2,1,0:T(8,128)S(1)}, u32[]{:S(2)}, u32[]{:S(2)}) collective-permute-start(f32[1,32,128]{2,1,0:T(8,128)S(1)} %get-tuple-element.145), channel_id=1, source_target_pairs={{0,1},{1,2},{2,3},{3,4},{4,5},{5,6},{6,7},{7,8},{8,9},{9,10},{10,1... | collective-permute-start | bytes 49160 | tf_op jit(solution)/shard_map/ppermute | solution.py:19
  104.2 10.6 %collective-permute-start.10 = (f32[1,32,128]{2,1,0:T(8,128)S(1)}, f32[1,32,128]{2,1,0:T(8,128)S(1)}, u32[]{:S(2)}, u32[]{:S(2)}) collective-permute-start(f32[1,32,128]{2,1,0:T(8,128)S(1)} %get-tuple-element.144), channel_id=1, source_target_pairs={{1,0},{2,1},{3,2},{4,3},{5,4},{6,5},{7,6},{8,7},{9,8},{10,9},{11,1... | collective-permute-start | bytes 49160 | tf_op jit(solution)/shard_map/ppermute | solution.py:21
  106.1 8.7 %collective-permute-start.11 = (f32[1,32,128]{2,1,0:T(8,128)S(1)}, f32[1,32,128]{2,1,0:T(8,128)S(1)}, u32[]{:S(2)}, u32[]{:S(2)}) collective-permute-start(f32[1,32,128]{2,1,0:T(8,128)S(1)} %get-tuple-element.143), channel_id=1, source_target_pairs={{0,1},{1,2},{2,3},{3,4},{4,5},{5,6},{6,7},{7,8},{8,9},{9,10},{10,1... | collective-permute-start | bytes 49160 | tf_op jit(solution)/shard_map/ppermute | solution.py:19
  118.1 14.2 %collective-permute-start.16 = (f32[1,32,128]{2,1,0:T(8,128)S(1)}, f32[1,32,128]{2,1,0:T(8,128)S(1)}, u32[]{:S(2)}, u32[]{:S(2)}) collective-permute-start(f32[1,32,128]{2,1,0:T(8,128)S(1)} %get-tuple-element.140), channel_id=1, source_target_pairs={{1,0},{2,1},{3,2},{4,3},{5,4},{6,5},{7,6},{8,7},{9,8},{10,9},{11,1... | collective-permute-start | bytes 49160 | tf_op jit(solution)/shard_map/ppermute | solution.py:21
  120.0 12.3 %collective-permute-start.17 = (f32[1,32,128]{2,1,0:T(8,128)S(1)}, f32[1,32,128]{2,1,0:T(8,128)S(1)}, u32[]{:S(2)}, u32[]{:S(2)}) collective-permute-start(f32[1,32,128]{2,1,0:T(8,128)S(1)} %get-tuple-element.139), channel_id=1, source_target_pairs={{0,1},{1,2},{2,3},{3,4},{4,5},{5,6},{6,7},{7,8},{8,9},{9,10},{10,1... | collective-permute-start | bytes 49160 | tf_op jit(solution)/shard_map/ppermute | solution.py:19
  125.2 16.4 %collective-permute-start.12 = (f32[1,32,128]{2,1,0:T(8,128)S(1)}, f32[1,32,128]{2,1,0:T(8,128)S(1)}, u32[]{:S(2)}, u32[]{:S(2)}) collective-permute-start(f32[1,32,128]{2,1,0:T(8,128)S(1)} %get-tuple-element.142), channel_id=1, source_target_pairs={{1,0},{2,1},{3,2},{4,3},{5,4},{6,5},{7,6},{8,7},{9,8},{10,9},{11,1... | collective-permute-start | bytes 49160 | tf_op jit(solution)/shard_map/ppermute | solution.py:21
  127.1 14.5 %collective-permute-start.13 = (f32[1,32,128]{2,1,0:T(8,128)S(1)}, f32[1,32,128]{2,1,0:T(8,128)S(1)}, u32[]{:S(2)}, u32[]{:S(2)}) collective-permute-start(f32[1,32,128]{2,1,0:T(8,128)S(1)} %get-tuple-element.141), channel_id=1, source_target_pairs={{0,1},{1,2},{2,3},{3,4},{4,5},{5,6},{6,7},{7,8},{8,9},{9,10},{10,1... | collective-permute-start | bytes 49160 | tf_op jit(solution)/shard_map/ppermute | solution.py:19
  134.1 7.6 %collective-permute-start.18 = (f32[1,32,128]{2,1,0:T(8,128)S(1)}, f32[1,32,128]{2,1,0:T(8,128)S(1)}, u32[]{:S(2)}, u32[]{:S(2)}) collective-permute-start(f32[1,32,128]{2,1,0:T(8,128)S(1)} %get-tuple-element.138), channel_id=1, source_target_pairs={{1,0},{2,1},{3,2},{4,3},{5,4},{6,5},{7,6},{8,7},{9,8},{10,9},{11,1... | collective-permute-start | bytes 49160 | tf_op jit(solution)/shard_map/ppermute | solution.py:21
  136.0 6.4 %collective-permute-start.19 = (f32[1,32,128]{2,1,0:T(8,128)S(1)}, f32[1,32,128]{2,1,0:T(8,128)S(1)}, u32[]{:S(2)}, u32[]{:S(2)}) collective-permute-start(f32[1,32,128]{2,1,0:T(8,128)S(1)} %get-tuple-element.137), channel_id=1, source_target_pairs={{0,1},{1,2},{2,3},{3,4},{4,5},{5,6},{6,7},{7,8},{8,9},{9,10},{10,1... | collective-permute-start | bytes 49160 | tf_op jit(solution)/shard_map/ppermute | solution.py:19
  145.3 435.6 %all-reduce.15.cloned.1.call-start = ((), (), s32[]{:S(2)}) async-start(), calls=%async_computation | async-start | bytes 1769472 | tf_op jit(solution)/shard_map/psum | solution.py:255
  293.7 5.4 collective-permute-start.21
  299.1 119.6 %collective-permute-start.22 = (bf16[1,4,64,128]{3,2,1,0:T(8,128)(2,1)S(1)}, bf16[1,4,64,128]{3,2,1,0:T(8,128)(2,1)S(1)}, u32[]{:S(2)}, u32[]{:S(2)}) collective-permute-start(bf16[1,4,64,128]{3,2,1,0:T(8,128)(2,1)S(1)} %get-tuple-element.129), channel_id=1, source_target_pairs={{0,1},{1,2},{2,3},{3,4},{4,5},{5,6},{6,7},{7,8},{8,9},{9,10},{10,1... | collective-permute-start | bytes 196616 | tf_op jit(solution)/shard_map/ppermute | solution.py:19
  315.5 103.2 %collective-permute-start.23 = (bf16[1,4,64,128]{3,2,1,0:T(8,128)(2,1)S(1)}, bf16[1,4,64,128]{3,2,1,0:T(8,128)(2,1)S(1)}, u32[]{:S(2)}, u32[]{:S(2)}) collective-permute-start(bf16[1,4,64,128]{3,2,1,0:T(8,128)(2,1)S(1)} %get-tuple-element.130), channel_id=1, source_target_pairs={{1,0},{2,1},{3,2},{4,3},{5,4},{6,5},{7,6},{8,7},{9,8},{10,9},{11,1... | collective-permute-start | bytes 196616 | tf_op jit(solution)/shard_map/ppermute | solution.py:21
  (60 other events, 304.2 us)
Sparse Core Ops, SparseCore 0:
  145.4 138.1 all-reduce.16
  297.1 283.7 all-reduce.14
where the time goes:
time: 591 us; the launch traced here: 590 us
  waiting for transfers between devices  299 us (51%)
  blocking collectives  133 us (23%)
  starting transfers between devices  94.6 us (16%)
  local copies, waits for them, and re-layouts  24.3 us (4%)
  between operations  18.9 us (3%)
  other arithmetic  10.4 us (2%)
  matrix products  9.01 us (2%)
    psum x1, waiting for transfers between devices, per_device(): lax.psum((kernel_part, head_part, bias_part), ('shot', 'tile'))  154 us
    unnamed x3, waiting for transfers between devices  136 us
    psum x1, blocking collectives, per_device(): lax.psum((kernel_part, head_part, bias_part), ('shot', 'tile'))  101 us
    ppermute x12, starting transfers between devices, padded_2(): lax.ppermute(tail, axis, [(i, (i + 1) % count) for i in range(ends)])  66 us
    all_gather x1, blocking collectives, per_device(): tile_speed = lax.all_gather(velocity, 'shot', axis=1, tiled=True)  32.4 us
    ppermute x12, starting transfers between devices, padded_2(): lax.ppermute(head, axis, [((i + 1) % count, i) for i in range(ends)])  28.5 us
    unnamed x128, local copies, waits for them, and re-layouts  12.5 us
  transfers between devices with their start and end apart: 26, of which 7 were waited for; matrix products, arithmetic and copies ran while one was open for 3% of the time, Pallas kernels for 0%

commit v1 on v0

--- a/solution.py
+++ b/solution.py
@@ -253,7 +253,7 @@
     grad_padded = jnp.pad(grad_edges, ((0, 0), (0, 0), (0, 0), (1, 1)))
     latent_grad = fold_children(transposed(grad_padded, kernel))
     kernel_grad, head_grad, bias_grad = lax.psum(
-        (kernel_part, head_part, bias_part), ("shot", "tile")
+        lax.psum((kernel_part, head_part, bias_part), "shot"), "tile"
     )
     return (latent_grad, kernel_grad, head_grad, bias_grad)
 

time: 591 us -> 731 us (1.24)
  waiting for transfers between devices: 299 us -> 441 us
    psum x1 -> x2, waiting for transfers between devices: 154 us -> 297 us  [the longest x1 276 us: per_device(): lax.psum(lax.psum((kernel_part, head_part, bias_part), 'shot'), 'tile')]
    psum x1 -> x2, blocking collectives: 101 us -> 98.4 us  [the longest x1 72 us: per_device(): lax.psum(lax.psum((kernel_part, head_part, bias_part), 'shot'), 'tile')]
    unnamed x3 -> x4, waiting for transfers between devices: 136 us -> 136 us
  transfers between devices with their start and end apart: 26 -> 27, of which waited for: 7 -> 8; matrix products, arithmetic and copies ran while one was open for 3% -> 2% of each run, Pallas kernels for 0% -> 0%
where the time goes in v1:
time: 731 us; the launch traced here: 729 us
  waiting for transfers between devices  441 us (60%)
  blocking collectives  131 us (18%)
  starting transfers between devices  94.6 us (13%)
  local copies, waits for them, and re-layouts  24.5 us (3%)
  between operations  18.7 us (3%)
  other arithmetic  10.4 us (1%)
  matrix products  9.01 us (1%)
    psum x1, waiting for transfers between devices, per_device(): lax.psum(lax.psum((kernel_part, head_part, bias_part), 'shot'), 'tile')  276 us
    unnamed x4, waiting for transfers between devices  136 us
    psum x1, blocking collectives, per_device(): lax.psum(lax.psum((kernel_part, head_part, bias_part), 'shot'), 'tile')  72 us
    ppermute x12, starting transfers between devices, padded_2(): lax.ppermute(tail, axis, [(i, (i + 1) % count) for i in range(ends)])  66 us
    all_gather x1, blocking collectives, per_device(): tile_speed = lax.all_gather(velocity, 'shot', axis=1, tiled=True)  32.4 us
    ppermute x12, starting transfers between devices, padded_2(): lax.ppermute(head, axis, [((i + 1) % count, i) for i in range(ends)])  28.5 us
    psum x1, blocking collectives, per_device(): lax.psum((kernel_part, head_part, bias_part), 'shot')  26.3 us
    psum x1, waiting for transfers between devices, per_device(): lax.psum((kernel_part, head_part, bias_part), 'shot')  20.2 us
  transfers between devices with their start and end apart: 27, of which 8 were waited for; matrix products, arithmetic and copies ran while one was open for 2% of the time, Pallas kernels for 0%

profile of v1, /device:TPU:1, one launch (start us, length us, event | category | flops | bytes accessed | tf_op | source)
XLA Modules:
  0.0 729.5 jit_solution(16486142928370814061)
XLA Ops:
  8.4 4.8 collective-permute-start.1
  15.3 5.2 collective-permute-start.5
  20.5 2.2 collective-permute-start.7
  26.8 2.4 collective-permute-start.3
  29.2 1.9 collective-permute-start.4
  31.4 5.0 collective-permute-done.4
  42.4 32.4 %all_gather.3 = f32[6,32,128]{2,0,1:T(8,128)S(1)} all-gather(f32[6,2,128]{2,0,1:T(8,128)S(1)} %multiply_add_fusion.2), channel_id=1, replica_groups=mesh['shot'=16,'tile'=32] {'shot'}, dimensions={1}, use_global_device_ids=true | all-gather | bytes 104448 | tf_op jit(solution)/shard_map/all_gather | solution.py:212
  74.9 5.3 collective-permute-start
  80.2 6.1 collective-permute-start.6
  86.4 1.9 collective-permute-start.14
  88.3 5.1 collective-permute-start.15
  97.1 5.7 collective-permute-start.9
  106.1 5.7 collective-permute-start.11
  120.0 5.1 collective-permute-start.17
  127.0 5.1 collective-permute-start.13
  136.0 5.5 collective-permute-start.19
  147.2 136.4 %all-reduce.21.cloned.1.call-done = f32[6,32,128]{2,1,0:T(8,128)} async-done(((f32[6,32,128]{2,1,0:T(8,128)}), f32[6,32,128]{2,1,0:T(8,128)}) %all-reduce.21.cloned.1.call-update) | async-done | bytes 98320
  297.0 2.0 collective-permute-done.21
  299.0 16.4 %collective-permute-start.22 = (bf16[1,4,64,128]{3,2,1,0:T(8,128)(2,1)S(1)}, bf16[1,4,64,128]{3,2,1,0:T(8,128)(2,1)S(1)}, u32[]{:S(2)}, u32[]{:S(2)}) collective-permute-start(bf16[1,4,64,128]{3,2,1,0:T(8,128)(2,1)S(1)} %get-tuple-element.131), channel_id=1, source_target_pairs={{0,1},{1,2},{2,3},{3,4},{4,5},{5,6},{6,7},{7,8},{8,9},{9,10},{10,1... | collective-permute-start | bytes 196616 | tf_op jit(solution)/shard_map/ppermute | solution.py:19
  317.6 26.3 %all-reduce.12 = (f32[64]{0:T(128)S(1)}, f32[64]{0:T(128)S(1)}) all-reduce(f32[64]{0:T(128)S(1)} %convolution_bitcast_fusion, f32[64]{0:T(128)S(1)} %get-tuple-element.48), channel_id=1, replica_groups=mesh['shot'=16,'tile'=32] {'shot'}, use_global_device_ids=true, to_apply=%region_8.9 | all-reduce | flops 128 | bytes 1024 | tf_op jit(solution)/shard_map/psum | solution.py:256
  344.0 72.0 %all-reduce.11 = (f32[64]{0:T(128)}, f32[64]{0:T(128)}) all-reduce(f32[64]{0:T(128)S(1)} %get-tuple-element.46, f32[64]{0:T(128)S(1)} %get-tuple-element.47), channel_id=1, replica_groups=mesh['shot'=16,'tile'=32] {'tile'}, use_global_device_ids=true, to_apply=%region_9.10 | all-reduce | flops 128 | bytes 1024 | tf_op jit(solution)/shard_map/psum | solution.py:255
  421.6 20.2 %all-reduce.17.cloned.1.call-done = f32[27,64,64]{2,1,0:T(8,128)} async-done(((f32[27,64,64]{2,1,0:T(8,128)}), f32[27,64,64]{2,1,0:T(8,128)}) %all-reduce.17.cloned.1.call-update) | async-done | bytes 442384 | tf_op jit(solution)/shard_map/psum | solution.py:256
  444.4 276.4 %all-reduce.19.cloned.1.call-done = f32[27,64,64]{2,1,0:T(8,128)} async-done(((f32[27,64,64]{2,1,0:T(8,128)}), f32[27,64,64]{2,1,0:T(8,128)}) %all-reduce.19.cloned.1.call-update) | async-done | bytes 442384 | tf_op jit(solution)/shard_map/psum | solution.py:255
  720.8 2.2 copy.316
  (268 shorter events, 59.1 us)
Async XLA Ops:
  7.2 276.4 %all-reduce.21.cloned.1.call-start = ((), (), s32[]{:S(2)}) async-start(), calls=%async_computation.2 | async-start | bytes 196608
  8.4 18.3 %collective-permute-start.1 = (bf16[6,1,64,128]{3,2,1,0:T(8,128)(2,1)S(1)}, bf16[6,1,64,128]{3,2,1,0:T(8,128)(2,1)S(1)}, u32[]{:S(2)}, u32[]{:S(2)}) collective-permute-start(bf16[6,1,64,128]{3,2,1,0:T(8,128)(2,1)S(1)} %copy.176), channel_id=1, source_target_pairs={{0,32},{32,64},{64,96},{96,128},{128,160},{160,192},{192,224},{224... | collective-permute-start | bytes 294920 | tf_op jit(solution)/shard_map/ppermute | solution.py:19
  13.3 13.5 %collective-permute-start.2 = (bf16[6,1,64,128]{3,2,1,0:T(8,128)(2,1)S(1)}, bf16[6,1,64,128]{3,2,1,0:T(8,128)(2,1)S(1)}, u32[]{:S(2)}, u32[]{:S(2)}) collective-permute-start(bf16[6,1,64,128]{3,2,1,0:T(8,128)(2,1)S(1)} %copy.176), channel_id=1, source_target_pairs={{32,0},{64,32},{96,64},{128,96},{160,128},{192,160},{224,192},{256... | collective-permute-start | bytes 294920 | tf_op jit(solution)/shard_map/ppermute | solution.py:21
  15.3 15.9 %collective-permute-start.5 = (f32[1,32,128]{2,1,0:T(8,128)S(1)}, f32[1,32,128]{2,1,0:T(8,128)S(1)}, u32[]{:S(2)}, u32[]{:S(2)}) collective-permute-start(f32[1,32,128]{2,1,0:T(8,128)S(1)} %get-tuple-element.150), channel_id=1, source_target_pairs={{1,0},{2,1},{3,2},{4,3},{5,4},{6,5},{7,6},{8,7},{9,8},{10,9},{11,1... | collective-permute-start | bytes 49160 | tf_op jit(solution)/shard_map/ppermute | solution.py:21
  20.5 10.6 %collective-permute-start.7 = (f32[1,32,128]{2,1,0:T(8,128)S(1)}, f32[1,32,128]{2,1,0:T(8,128)S(1)}, u32[]{:S(2)}, u32[]{:S(2)}) collective-permute-start(f32[1,32,128]{2,1,0:T(8,128)S(1)} %get-tuple-element.149), channel_id=1, source_target_pairs={{0,1},{1,2},{2,3},{3,4},{4,5},{5,6},{6,7},{7,8},{8,9},{9,10},{10,1... | collective-permute-start | bytes 49160 | tf_op jit(solution)/shard_map/ppermute | solution.py:19
  29.2 7.1 collective-permute-start.4
  74.9 18.6 %collective-permute-start = (f32[1,32,128]{2,1,0:T(8,128)S(1)}, f32[1,32,128]{2,1,0:T(8,128)S(1)}, u32[]{:S(2)}, u32[]{:S(2)}) collective-permute-start(f32[1,32,128]{2,1,0:T(8,128)S(1)} %get-tuple-element.152), channel_id=1, source_target_pairs={{1,0},{2,1},{3,2},{4,3},{5,4},{6,5},{7,6},{8,7},{9,8},{10,9},{11,1... | collective-permute-start | bytes 49160 | tf_op jit(solution)/shard_map/ppermute | solution.py:21
  80.2 13.3 %collective-permute-start.6 = (f32[1,32,128]{2,1,0:T(8,128)S(1)}, f32[1,32,128]{2,1,0:T(8,128)S(1)}, u32[]{:S(2)}, u32[]{:S(2)}) collective-permute-start(f32[1,32,128]{2,1,0:T(8,128)S(1)} %get-tuple-element.151), channel_id=1, source_target_pairs={{0,1},{1,2},{2,3},{3,4},{4,5},{5,6},{6,7},{7,8},{8,9},{9,10},{10,1... | collective-permute-start | bytes 49160 | tf_op jit(solution)/shard_map/ppermute | solution.py:19
  86.4 7.3 collective-permute-start.14
  88.3 6.0 collective-permute-start.15
  95.1 8.4 %collective-permute-start.8 = (f32[1,32,128]{2,1,0:T(8,128)S(1)}, f32[1,32,128]{2,1,0:T(8,128)S(1)}, u32[]{:S(2)}, u32[]{:S(2)}) collective-permute-start(f32[1,32,128]{2,1,0:T(8,128)S(1)} %get-tuple-element.148), channel_id=1, source_target_pairs={{1,0},{2,1},{3,2},{4,3},{5,4},{6,5},{7,6},{8,7},{9,8},{10,9},{11,1... | collective-permute-start | bytes 49160 | tf_op jit(solution)/shard_map/ppermute | solution.py:21
  97.1 6.6 collective-permute-start.9
  104.2 10.6 %collective-permute-start.10 = (f32[1,32,128]{2,1,0:T(8,128)S(1)}, f32[1,32,128]{2,1,0:T(8,128)S(1)}, u32[]{:S(2)}, u32[]{:S(2)}) collective-permute-start(f32[1,32,128]{2,1,0:T(8,128)S(1)} %get-tuple-element.146), channel_id=1, source_target_pairs={{1,0},{2,1},{3,2},{4,3},{5,4},{6,5},{7,6},{8,7},{9,8},{10,9},{11,1... | collective-permute-start | bytes 49160 | tf_op jit(solution)/shard_map/ppermute | solution.py:21
  106.1 8.7 %collective-permute-start.11 = (f32[1,32,128]{2,1,0:T(8,128)S(1)}, f32[1,32,128]{2,1,0:T(8,128)S(1)}, u32[]{:S(2)}, u32[]{:S(2)}) collective-permute-start(f32[1,32,128]{2,1,0:T(8,128)S(1)} %get-tuple-element.145), channel_id=1, source_target_pairs={{0,1},{1,2},{2,3},{3,4},{4,5},{5,6},{6,7},{7,8},{8,9},{9,10},{10,1... | collective-permute-start | bytes 49160 | tf_op jit(solution)/shard_map/ppermute | solution.py:19
  118.0 14.2 %collective-permute-start.16 = (f32[1,32,128]{2,1,0:T(8,128)S(1)}, f32[1,32,128]{2,1,0:T(8,128)S(1)}, u32[]{:S(2)}, u32[]{:S(2)}) collective-permute-start(f32[1,32,128]{2,1,0:T(8,128)S(1)} %get-tuple-element.142), channel_id=1, source_target_pairs={{1,0},{2,1},{3,2},{4,3},{5,4},{6,5},{7,6},{8,7},{9,8},{10,9},{11,1... | collective-permute-start | bytes 49160 | tf_op jit(solution)/shard_map/ppermute | solution.py:21
  120.0 12.3 %collective-permute-start.17 = (f32[1,32,128]{2,1,0:T(8,128)S(1)}, f32[1,32,128]{2,1,0:T(8,128)S(1)}, u32[]{:S(2)}, u32[]{:S(2)}) collective-permute-start(f32[1,32,128]{2,1,0:T(8,128)S(1)} %get-tuple-element.141), channel_id=1, source_target_pairs={{0,1},{1,2},{2,3},{3,4},{4,5},{5,6},{6,7},{7,8},{8,9},{9,10},{10,1... | collective-permute-start | bytes 49160 | tf_op jit(solution)/shard_map/ppermute | solution.py:19
  125.1 16.4 %collective-permute-start.12 = (f32[1,32,128]{2,1,0:T(8,128)S(1)}, f32[1,32,128]{2,1,0:T(8,128)S(1)}, u32[]{:S(2)}, u32[]{:S(2)}) collective-permute-start(f32[1,32,128]{2,1,0:T(8,128)S(1)} %get-tuple-element.144), channel_id=1, source_target_pairs={{1,0},{2,1},{3,2},{4,3},{5,4},{6,5},{7,6},{8,7},{9,8},{10,9},{11,1... | collective-permute-start | bytes 49160 | tf_op jit(solution)/shard_map/ppermute | solution.py:21
  127.0 14.5 %collective-permute-start.13 = (f32[1,32,128]{2,1,0:T(8,128)S(1)}, f32[1,32,128]{2,1,0:T(8,128)S(1)}, u32[]{:S(2)}, u32[]{:S(2)}) collective-permute-start(f32[1,32,128]{2,1,0:T(8,128)S(1)} %get-tuple-element.143), channel_id=1, source_target_pairs={{0,1},{1,2},{2,3},{3,4},{4,5},{5,6},{6,7},{7,8},{8,9},{9,10},{10,1... | collective-permute-start | bytes 49160 | tf_op jit(solution)/shard_map/ppermute | solution.py:19
  134.1 7.6 %collective-permute-start.18 = (f32[1,32,128]{2,1,0:T(8,128)S(1)}, f32[1,32,128]{2,1,0:T(8,128)S(1)}, u32[]{:S(2)}, u32[]{:S(2)}) collective-permute-start(f32[1,32,128]{2,1,0:T(8,128)S(1)} %get-tuple-element.140), channel_id=1, source_target_pairs={{1,0},{2,1},{3,2},{4,3},{5,4},{6,5},{7,6},{8,7},{9,8},{10,9},{11,1... | collective-permute-start | bytes 49160 | tf_op jit(solution)/shard_map/ppermute | solution.py:21
  136.0 6.4 collective-permute-start.19
  145.2 296.5 %all-reduce.17.cloned.1.call-start = ((), (), s32[]{:S(2)}) async-start(), calls=%async_computation | async-start | bytes 1769472 | tf_op jit(solution)/shard_map/psum | solution.py:256
  296.9 423.8 %all-reduce.19.cloned.1.call-start = ((), (), s32[]{:S(2)}) async-start(), calls=%async_computation.1 | async-start | bytes 1769472 | tf_op jit(solution)/shard_map/psum | solution.py:255
  299.0 117.0 %collective-permute-start.22 = (bf16[1,4,64,128]{3,2,1,0:T(8,128)(2,1)S(1)}, bf16[1,4,64,128]{3,2,1,0:T(8,128)(2,1)S(1)}, u32[]{:S(2)}, u32[]{:S(2)}) collective-permute-start(bf16[1,4,64,128]{3,2,1,0:T(8,128)(2,1)S(1)} %get-tuple-element.131), channel_id=1, source_target_pairs={{0,1},{1,2},{2,3},{3,4},{4,5},{5,6},{6,7},{7,8},{8,9},{9,10},{10,1... | collective-permute-start | bytes 196616 | tf_op jit(solution)/shard_map/ppermute | solution.py:19
  315.5 100.6 %collective-permute-start.23 = (bf16[1,4,64,128]{3,2,1,0:T(8,128)(2,1)S(1)}, bf16[1,4,64,128]{3,2,1,0:T(8,128)(2,1)S(1)}, u32[]{:S(2)}, u32[]{:S(2)}) collective-permute-start(bf16[1,4,64,128]{3,2,1,0:T(8,128)(2,1)S(1)} %get-tuple-element.132), channel_id=1, source_target_pairs={{1,0},{2,1},{3,2},{4,3},{5,4},{6,5},{7,6},{8,7},{9,8},{10,9},{11,1... | collective-permute-start | bytes 196616 | tf_op jit(solution)/shard_map/ppermute | solution.py:21
  (61 other events, 329.0 us)
Sparse Core Ops, SparseCore 0:
  145.3 138.1 all-reduce.20
  297.1 144.6 all-reduce.16
  444.7 276.0 all-reduce.18
